TPU v7x, 256 devices: a whole 4x4x8 slice. The times are simulated.
256 devices in a mesh: blk: 32 (over y, z), head: 2 (over core), clip: 4 (over x).
Axes of the slice: x: 4, y: 4, z: 8, core: 2. Of those that a mesh axis runs over, the one named last changes fastest.
Arguments:
- tokens: bfloat16 [36864, 1536], P(('clip', 'blk', 'head')), parts along dimension 0, may hold values from -6 to 6
- modulation: float32 [12, 1536], P('clip'), parts along dimension 0, may hold values from -3 to 3
- w_qkv: bfloat16 [1536, 3, 1536], P(None, None, 'head'), may hold values from -0.25 to 0.25
- w_out: bfloat16 [1536, 1536], P('head'), may hold values from -0.15625 to 0.15625
- w_cross: bfloat16 [1536, 1536], P(None, 'head'), may hold values from -0.15625 to 0.15625
- q_gain: float32 [128], replicated, may hold values from 0.5 to 6
- k_gain: float32 [128], replicated, may hold values from 0.5 to 6
- cross_gain: float32 [128], replicated, may hold values from 0.5 to 6
- scene_keys: bfloat16 [8192, 1536], P(('clip', 'blk'), 'head'), parts along dimension 0, may hold values from -40 to 40
- scene_values: bfloat16 [8192, 1536], P(('clip', 'blk'), 'head'), parts along dimension 0, may hold values from -6 to 6
Outputs:
- hidden: bfloat16 [36864, 1536], P(('clip', 'blk', 'head')), parts along dimension 0
- cross_context: bfloat16 [36864, 1536], P(('clip', 'blk'), 'head'), parts along dimension 0
There are 4 independent parts, one for each index of `clip`. A program takes and returns all parts, laid end to end along the dimension named above; an argument that names none is the same for every part. Nothing has to cross between parts.
All inputs are finite; a program needn't handle non-finite values.
Results may differ from a plain program's by a relative error of at most 0.015.
The roundings to bfloat16 on the way count: a program that leaves them out, or rounds other values in their place, can miss the bound.
Values may be sent and summed in bfloat16 or wider, within the bound.
A program may use at most 128 MiB of HBM per device.

v0:
```python
import jax
import jax.numpy as jnp
from jax import lax
from jax.sharding import PartitionSpec as P

HD = 128


def head_norm(values, gain):
    rms = jnp.mean(values * values, axis=-1, keepdims=True)
    return values * lax.rsqrt(rms + 1e-06) * gain


def attend_block(carry, queries, keys_blk, values_blk):
    best, total, accum = carry
    count = keys_blk.shape[0]
    heads_here = queries.shape[1]
    width = queries.shape[2]
    keys_three = keys_blk.reshape(count, heads_here, width)
    values_three = values_blk.reshape(count, heads_here, width).astype(jnp.float32)
    scores = jnp.einsum("rhd,nhd->hrn", queries, keys_three, preferred_element_type=jnp.float32) * (
        1.0 / width**0.5
    )
    newbest = jnp.maximum(best, jnp.max(scores, axis=-1))
    factor = jnp.exp(best - newbest)
    weights = jnp.exp(scores - newbest[..., None])
    total = total * factor + jnp.sum(weights, axis=-1)
    accum = accum * jnp.transpose(factor)[..., None] + jnp.einsum(
        "hrn,nhd->rhd", weights, values_three
    )
    return (newbest, total, accum)


def attend_keys(carry, queries, keys_rows, values_rows):
    count = keys_rows.shape[0]
    blocks = count // 1024
    keys_split = keys_rows.reshape(blocks, 1024, keys_rows.shape[1])
    values_split = values_rows.reshape(blocks, 1024, values_rows.shape[1])

    def advance(state, pair):
        return (attend_block(state, queries, pair[0], pair[1]), None)

    carry, unused = lax.scan(advance, carry, (keys_split, values_split))
    return carry


def start_state(queries):
    rows = queries.shape[0]
    heads_here = queries.shape[1]
    best = jnp.full((heads_here, rows), -1e30, jnp.float32)
    total = jnp.zeros((heads_here, rows), jnp.float32)
    accum = jnp.zeros(queries.shape, jnp.float32)
    return (best, total, accum)


def finish_state(state):
    best, total, accum = state
    result = accum / jnp.transpose(total)[..., None]
    return result.reshape(result.shape[0], result.shape[1] * result.shape[2]).astype(jnp.bfloat16)


def shards(
    tokens, modulation, w_qkv, w_out, w_cross, q_gain, k_gain, cross_gain, scene_keys, scene_values
):
    width = tokens.shape[1]
    local_width = w_qkv.shape[2]
    heads_here = local_width // HD
    rows_raw = lax.all_gather(tokens, "head", axis=0, tiled=True)
    rows_count = rows_raw.shape[0]
    xfloat = rows_raw.astype(jnp.float32)
    mean = jnp.mean(xfloat, axis=-1, keepdims=True)
    var = jnp.mean((xfloat - mean) ** 2, axis=-1, keepdims=True)
    normed = (xfloat - mean) * lax.rsqrt(var + 1e-06)
    modulated = (normed * (1.0 + modulation[1]) + modulation[0]).astype(jnp.bfloat16)
    projected = jnp.dot(
        modulated, w_qkv.reshape(width, 3 * local_width), preferred_element_type=jnp.float32
    )
    projected = projected.reshape(rows_count, 3, heads_here, HD)
    queries = head_norm(projected[:, 0], q_gain).astype(jnp.bfloat16)
    keys_flat = (
        head_norm(projected[:, 1], k_gain).astype(jnp.bfloat16).reshape(rows_count, local_width)
    )
    values_flat = projected[:, 2].astype(jnp.bfloat16).reshape(rows_count, local_width)
    pieces = (
        lax.all_gather(keys_flat, "blk", axis=0, tiled=True),
        lax.all_gather(values_flat, "blk", axis=0, tiled=True),
    )
    state = attend_keys(start_state(queries), queries, pieces[0], pieces[1])
    context = finish_state(state)
    partial_sum = jnp.dot(context, w_out, preferred_element_type=jnp.float32)
    mine = lax.psum_scatter(partial_sum, "head", scatter_dimension=0, tiled=True)
    hidden = (tokens.astype(jnp.float32) + modulation[2] * mine).astype(jnp.bfloat16)
    hidden_all = lax.all_gather(hidden, "head", axis=0, tiled=True)
    cross_proj = jnp.dot(hidden_all, w_cross, preferred_element_type=jnp.float32).reshape(
        rows_count, heads_here, HD
    )
    cross_queries = head_norm(cross_proj, cross_gain).astype(jnp.bfloat16)
    pieces = (
        lax.all_gather(scene_keys, "blk", axis=0, tiled=True),
        lax.all_gather(scene_values, "blk", axis=0, tiled=True),
    )
    scene_state = attend_keys(start_state(cross_queries), cross_queries, pieces[0], pieces[1])
    cross_context = finish_state(scene_state)
    return (hidden, cross_context)


def solution(mesh):
    return jax.shard_map(
        shards,
        mesh=mesh,
        in_specs=(
            P(("clip", "blk", "head"), None),
            P("clip", None),
            P(None, None, "head"),
            P("head", None),
            P(None, "head"),
            P(),
            P(),
            P(),
            P(("clip", "blk"), "head"),
            P(("clip", "blk"), "head"),
        ),
        out_specs=(P(("clip", "blk", "head"), None), P(("clip", "blk"), "head")),
        check_vma=False,
    )
```

profile of v0, /device:TPU:2, one launch (start us, length us, event | category | flops | bytes accessed | tf_op | source)
XLA Modules:
  0.0 703.8 jit_solution(5438818760283527297)
XLA Ops:
  10.7 10.3 %copy.64 = bf16[1536,3,768]{0,2,1:T(8,128)(2,1)} copy(bf16[1536,3,768]{2,0,1:T(8,128)(2,1)} %param.16) | data formatting | bytes 14155776 | tf_op args[2]
  21.0 5.0 fusion.37
  36.4 124.1 %all-gather.5.cloned.1.call-done = bf16[9216,768]{1,0:T(8,128)(2,1)} async-done(((bf16[288,768]{1,0:T(8,128)(2,1)}), bf16[9216,768]{1,0:T(8,128)(2,1)}) %all-gather.5.cloned.1.call-update) | async-done | bytes 14155792 | tf_op jit(solution)/shard_map/all_gather | solution.py:85
  160.4 126.9 %all-gather.7.cloned.1.call-done = bf16[9216,768]{1,0:T(8,128)(2,1)} async-done(((bf16[288,768]{1,0:T(8,128)(2,1)}), bf16[9216,768]{1,0:T(8,128)(2,1)}) %all-gather.7.cloned.1.call-update) | async-done | bytes 14155792 | tf_op jit(solution)/shard_map/all_gather | solution.py:86
  287.3 194.9 %while.30 = (s32[]{:T(128)}, f32[6,288]{1,0:T(8,128)S(1)}, f32[6,288]{1,0:T(8,128)S(1)}, f32[288,6,128]{2,0,1:T(8,128)S(1)}, bf16[9,1024,768]{2,1,0:T(8,128)(2,1...) while((s32[]{:T(128)}, f32[6,288]{1,0:T(8,128)S(1)}, ...), condition=%wide.region_7.8_spmd.clone, body=%wide.region_4.7_spmd.clone.sunk | while | flops 919029888 | bytes 67596424 | solution.py:43
  293.7 5.5 bitcast_reduce_fusion.4
  315.3 5.5 bitcast_reduce_fusion.4
  323.4 4.7 fusion.88
  337.0 5.5 bitcast_reduce_fusion.4
  345.1 4.7 fusion.88
  358.6 5.5 bitcast_reduce_fusion.4
  366.7 4.7 fusion.88
  380.3 5.5 bitcast_reduce_fusion.4
  402.0 5.5 bitcast_reduce_fusion.4
  410.0 4.7 fusion.88
  423.6 5.5 bitcast_reduce_fusion.4
  431.7 4.7 fusion.88
  445.3 5.5 bitcast_reduce_fusion.4
  453.4 4.7 fusion.88
  466.9 5.5 bitcast_reduce_fusion.4
  485.6 10.6 %reduce-scatter.2.cloned.1.call-done = f32[144,1536]{1,0:T(8,128)} async-done(((f32[288,1536]{1,0:T(8,128)}), f32[144,1536]{1,0:T(8,128)}) %reduce-scatter.2.cloned.1.call-update) | async-done | bytes 884752 | tf_op jit(solution)/shard_map/reduce_scatter | solution.py:91
  504.0 76.2 %all-gather.9.cloned.1.call-done = bf16[2048,768]{1,0:T(8,128)(2,1)} async-done(((bf16[64,768]{1,0:T(8,128)(2,1)}), bf16[2048,768]{1,0:T(8,128)(2,1)}) %all-gather.9.cloned.1.call-update) | async-done | bytes 3145744 | tf_op jit(solution)/shard_map/all_gather | solution.py:99
  580.2 79.4 %all-gather.11.cloned.1.call-done = bf16[2048,768]{1,0:T(8,128)(2,1)} async-done(((bf16[64,768]{1,0:T(8,128)(2,1)}), bf16[2048,768]{1,0:T(8,128)(2,1)}) %all-gather.11.cloned.1.call-update) | async-done | bytes 3145744 | tf_op jit(solution)/shard_map/all_gather | solution.py:100
  659.6 35.9 %while.31 = (s32[]{:T(128)}, f32[6,288]{1,0:T(8,128)S(1)}, f32[6,288]{1,0:T(8,128)S(1)}, f32[288,6,128]{2,0,1:T(8,128)S(1)}, bf16[2,1024,768]{2,1,0:T(8,128)(2,1...) while((s32[]{:T(128)}, f32[6,288]{1,0:T(8,128)S(1)}, ...), condition=%wide.region_13.14_spmd.clone, body=%wide.region_10.13_spmd.clone.sunk | while | flops 919029888 | bytes 67596424 | solution.py:43
  (169 shorter events, 179.3 us)
Async XLA Ops:
  7.2 475.1 %copy-start = (bf16[768,1536]{1,0:T(8,128)(2,1)S(1)}, bf16[768,1536]{1,0:T(8,128)(2,1)}, u32[]{:S(2)}) copy-start(bf16[768,1536]{1,0:T(8,128)(2,1)} %param.17) | copy-start | bytes 7077892
  7.2 3.5 copy-start.6
  7.2 153.3 %all-gather.5.cloned.1.call-start = ((), (), s32[]{:S(2)}) async-start(), calls=%async_computation.1 | async-start | bytes 14598144 | tf_op jit(solution)/shard_map/all_gather | solution.py:85
  26.0 1.6 copy-start.4
  27.6 1.1 copy-start.9
  30.1 4.0 copy-start.7
  30.1 257.2 %all-gather.7.cloned.1.call-start = ((), (), s32[]{:S(2)}) async-start(), calls=%async_computation.2 | async-start | bytes 14598144 | tf_op jit(solution)/shard_map/all_gather | solution.py:86
  32.5 463.7 %reduce-scatter.2.cloned.1.call-start = ((), (), s32[]{:S(2)}) async-start(), calls=%async_computation.3 | async-start | bytes 2654208 | tf_op jit(solution)/shard_map/reduce_scatter | solution.py:91
  301.8 5.5 copy-start.2
  323.4 5.5 copy-start.2
  345.1 5.5 copy-start.2
  366.7 5.5 copy-start.2
  388.4 5.5 copy-start.2
  410.0 5.5 copy-start.2
  431.7 5.5 copy-start.2
  453.4 5.5 copy-start.2
  475.0 5.5 copy-start.2
  484.4 95.8 %all-gather.9.cloned.1.call-start = ((), (), s32[]{:S(2)}) async-start(), calls=%async_computation.4 | async-start | bytes 3244032 | tf_op jit(solution)/shard_map/all_gather | solution.py:99
  485.0 174.6 %all-gather.11.cloned.1.call-start = ((), (), s32[]{:S(2)}) async-start(), calls=%async_computation.5 | async-start | bytes 3244032 | tf_op jit(solution)/shard_map/all_gather | solution.py:100
  497.6 2.6 copy-start.5
  502.8 0.8 copy-start.8
  670.8 5.1 copy-start.3
  688.7 5.1 copy-start.3
  695.5 1.8 copy-start.1
Sparse Core Ops, SparseCore 0:
  30.3 130.1 all-gather.4
  163.0 124.2 all-gather.6
  484.5 11.6 reduce-scatter.1
  499.0 81.1 all-gather.8
  583.0 76.5 all-gather.10
where the time goes:
time: 705 us; the launch traced here: 704 us
  waiting for transfers between devices  418 us (59%)
  local copies, waits for them, and re-layouts  120 us (17%)
  matrix products  118 us (17%)
  other arithmetic  27.2 us (4%)
  between operations  14.1 us (2%)
    all_gather x1, waiting for transfers between devices, shards(): lax.all_gather(values_flat, 'blk', axis=0, tiled=True)  127 us
    all_gather x1, waiting for transfers between devices, shards(): lax.all_gather(keys_flat, 'blk', axis=0, tiled=True)  124 us
    dynamic_slice x33, local copies, waits for them, and re-layouts, attend_keys(): carry, unused = lax.scan(advance, carry, (keys_split, values_split))  94.9 us
    all_gather x1, waiting for transfers between devices, shards(): lax.all_gather(scene_values, 'blk', axis=0, tiled=True)  79.4 us
    all_gather x1, waiting for transfers between devices, shards(): lax.all_gather(scene_keys, 'blk', axis=0, tiled=True)  76.2 us
    dot_general x11, matrix products, attend_block(): jnp.einsum('rhd,nhd->hrn', queries, keys_three, preferred_element_type=jn...  57.3 us
    dot_general x11, matrix products, attend_block(): jnp.einsum('hrn,nhd->rhd', weights, values_three)  51.1 us
    reduce_sum x11, other arithmetic, attend_block(): total = total * factor + jnp.sum(weights, axis=-1)  17.8 us
  transfers between devices with their start and end apart: 5, of which 5 were waited for; matrix products, arithmetic and copies ran while one was open for 2% of the time, Pallas kernels for 0%

commit v1 on v0

--- a/solution.py
+++ b/solution.py
@@ -97,7 +97,9 @@
     cross_queries = head_norm(cross_proj, cross_gain).astype(jnp.bfloat16)
     pieces = (
         lax.all_gather(scene_keys, "blk", axis=0, tiled=True),
-        lax.all_gather(scene_values, "blk", axis=0, tiled=True),
+        jnp.concatenate(
+            lax.all_to_all(jnp.stack([scene_values] * lax.axis_size("blk")), "blk", 0, 0), axis=0
+        ),
     )
     scene_state = attend_keys(start_state(cross_queries), cross_queries, pieces[0], pieces[1])
     cross_context = finish_state(scene_state)

time: 705 us -> 636 us (0.902)
  waiting for transfers between devices: 418 us -> 343 us
    all_gather x1 -> x0, waiting for transfers between devices: 79.4 us -> none  [shards(): lax.all_gather(scene_values, 'blk', axis=0, tiled=True)]
    all_to_all x0 -> x1, waiting for transfers between devices: none -> 70.4 us  [shards(): lax.all_to_all(jnp.stack([scene_values] * lax.axis_size('blk')), 'blk', 0...]
    all_gather x1, waiting for transfers between devices: 76.2 us -> 17.4 us  [shards(): lax.all_gather(scene_keys, 'blk', axis=0, tiled=True)]
    reduce_scatter x1, waiting for transfers between devices: 10.6 us -> 3.33 us  [shards(): lax.psum_scatter(partial_sum, 'head', scatter_dimension=0, tiled=True)]
where the time goes in v1:
time: 636 us; the launch traced here: 634 us
  waiting for transfers between devices  343 us (54%)
  local copies, waits for them, and re-layouts  122 us (19%)
  matrix products  116 us (18%)
  other arithmetic  27.2 us (4%)
  between operations  14.1 us (2%)
    all_gather x1, waiting for transfers between devices, shards(): lax.all_gather(values_flat, 'blk', axis=0, tiled=True)  127 us
    all_gather x1, waiting for transfers between devices, shards(): lax.all_gather(keys_flat, 'blk', axis=0, tiled=True)  124 us
    dynamic_slice x33, local copies, waits for them, and re-layouts, attend_keys(): carry, unused = lax.scan(advance, carry, (keys_split, values_split))  94.9 us
    all_to_all x1, waiting for transfers between devices, shards(): lax.all_to_all(jnp.stack([scene_values] * lax.axis_size('blk')), 'blk', 0...  70.4 us
    dot_general x11, matrix products, attend_block(): jnp.einsum('rhd,nhd->hrn', queries, keys_three, preferred_element_type=jn...  57.3 us
    dot_general x11, matrix products, attend_block(): jnp.einsum('hrn,nhd->rhd', weights, values_three)  51.1 us
    reduce_sum x11, other arithmetic, attend_block(): total = total * factor + jnp.sum(weights, axis=-1)  17.8 us
    all_gather x1, waiting for transfers between devices, shards(): lax.all_gather(scene_keys, 'blk', axis=0, tiled=True)  17.4 us
  transfers between devices with their start and end apart: 5, of which 5 were waited for; matrix products, arithmetic and copies ran while one was open for 2% of the time, Pallas kernels for 0%

profile of v1, /device:TPU:2, one launch (start us, length us, event | category | flops | bytes accessed | tf_op | source)
XLA Modules:
  0.0 634.4 jit_solution(8511148220994235086)
XLA Ops:
  10.7 10.3 %copy.64 = bf16[1536,3,768]{0,2,1:T(8,128)(2,1)} copy(bf16[1536,3,768]{2,0,1:T(8,128)(2,1)} %param.16) | data formatting | bytes 14155776 | tf_op args[2]
  21.0 5.0 fusion.37
  36.4 124.1 %all-gather.4.cloned.1.call-done = bf16[9216,768]{1,0:T(8,128)(2,1)} async-done(((bf16[288,768]{1,0:T(8,128)(2,1)}), bf16[9216,768]{1,0:T(8,128)(2,1)}) %all-gather.4.cloned.1.call-update) | async-done | bytes 14155792 | tf_op jit(solution)/shard_map/all_gather | solution.py:85
  160.4 126.9 %all-gather.6.cloned.1.call-done = bf16[9216,768]{1,0:T(8,128)(2,1)} async-done(((bf16[288,768]{1,0:T(8,128)(2,1)}), bf16[9216,768]{1,0:T(8,128)(2,1)}) %all-gather.6.cloned.1.call-update) | async-done | bytes 14155792 | tf_op jit(solution)/shard_map/all_gather | solution.py:86
  287.3 194.9 %while.30 = (s32[]{:T(128)}, f32[6,288]{1,0:T(8,128)S(1)}, f32[6,288]{1,0:T(8,128)S(1)}, f32[288,6,128]{2,0,1:T(8,128)S(1)}, bf16[9,1024,768]{2,1,0:T(8,128)(2,1...) while((s32[]{:T(128)}, f32[6,288]{1,0:T(8,128)S(1)}, ...), condition=%wide.region_7.8_spmd.clone, body=%wide.region_4.7_spmd.clone.sunk | while | flops 919029888 | bytes 67596424 | solution.py:43
  293.7 5.5 bitcast_reduce_fusion.4
  315.3 5.5 bitcast_reduce_fusion.4
  323.4 4.7 fusion.88
  337.0 5.5 bitcast_reduce_fusion.4
  345.1 4.7 fusion.88
  358.6 5.5 bitcast_reduce_fusion.4
  366.7 4.7 fusion.88
  380.3 5.5 bitcast_reduce_fusion.4
  402.0 5.5 bitcast_reduce_fusion.4
  410.0 4.7 fusion.88
  423.6 5.5 bitcast_reduce_fusion.4
  431.7 4.7 fusion.88
  445.3 5.5 bitcast_reduce_fusion.4
  453.4 4.7 fusion.88
  466.9 5.5 bitcast_reduce_fusion.4
  486.4 5.9 all-to-all-start
  502.4 70.4 %all-to-all-done = bf16[32,64,768]{2,1,0:T(8,128)(2,1)} async-done(((bf16[32,64,768]{2,1,0:T(8,128)(2,1)}), bf16[32,64,768]{2,1,0:T(8,128)(2,1)}, u32[]{:S(2)}, u32[]{:S(2)}) %all-to-all-start) | async-done | bytes 3145760 | tf_op jit(solution)/shard_map/all_to_all | solution.py:101
  572.8 17.4 %all-gather.8.cloned.1.call-done = bf16[2048,768]{1,0:T(8,128)(2,1)} async-done(((bf16[64,768]{1,0:T(8,128)(2,1)}), bf16[2048,768]{1,0:T(8,128)(2,1)}) %all-gather.8.cloned.1.call-update) | async-done | bytes 3145744 | tf_op jit(solution)/shard_map/all_gather | solution.py:99
  590.2 35.9 %while.31 = (s32[]{:T(128)}, f32[6,288]{1,0:T(8,128)S(1)}, f32[6,288]{1,0:T(8,128)S(1)}, f32[288,6,128]{2,0,1:T(8,128)S(1)}, bf16[2,1024,768]{2,1,0:T(8,128)(2,1...) while((s32[]{:T(128)}, f32[6,288]{1,0:T(8,128)S(1)}, ...), condition=%wide.region_13.14_spmd.clone, body=%wide.region_10.13_spmd.clone.sunk | while | flops 919029888 | bytes 67596424 | solution.py:43
  (175 shorter events, 182.5 us)
Async XLA Ops:
  7.2 475.1 %copy-start = (bf16[768,1536]{1,0:T(8,128)(2,1)S(1)}, bf16[768,1536]{1,0:T(8,128)(2,1)}, u32[]{:S(2)}) copy-start(bf16[768,1536]{1,0:T(8,128)(2,1)} %param.17) | copy-start | bytes 7077892
  7.2 3.5 copy-start.8
  7.2 153.3 %all-gather.4.cloned.1.call-start = ((), (), s32[]{:S(2)}) async-start(), calls=%async_computation.2 | async-start | bytes 14598144 | tf_op jit(solution)/shard_map/all_gather | solution.py:85
  30.1 4.0 copy-start.9
  30.1 257.2 %all-gather.6.cloned.1.call-start = ((), (), s32[]{:S(2)}) async-start(), calls=%async_computation.3 | async-start | bytes 14598144 | tf_op jit(solution)/shard_map/all_gather | solution.py:86
  32.5 463.8 %reduce-scatter.2.cloned.1.call-start = ((), (), s32[]{:S(2)}) async-start(), calls=%async_computation.4 | async-start | bytes 2654208 | tf_op jit(solution)/shard_map/reduce_scatter | solution.py:91
  301.8 5.5 copy-start.2
  323.4 5.5 copy-start.2
  345.1 5.5 copy-start.2
  366.7 5.5 copy-start.2
  388.4 5.5 copy-start.2
  410.0 5.5 copy-start.2
  431.7 5.5 copy-start.2
  453.4 5.5 copy-start.2
  475.0 5.5 copy-start.2
  482.2 2.2 copy-start.7
  486.4 9.8 %copy-start.5 = (bf16[144,1536]{1,0:T(8,128)(2,1)S(1)}, bf16[144,1536]{1,0:T(8,128)(2,1)}, u32[]{:S(2)}) copy-start(bf16[144,1536]{1,0:T(8,128)(2,1)} %param.14) | copy-start | bytes 1327108
  486.4 86.4 %all-to-all-start = ((bf16[32,64,768]{2,1,0:T(8,128)(2,1)}), bf16[32,64,768]{2,1,0:T(8,128)(2,1)}, u32[]{:S(2)}, u32[]{:S(2)}) async-start(bf16[32,64,768]{2,1,0:T(8,128)(2,1)} %stack.2), calls=%async_computation.1 | async-start | bytes 6291456 | tf_op jit(solution)/shard_map/all_to_all | solution.py:101
  492.3 97.9 %all-gather.8.cloned.1.call-start = ((), (), s32[]{:S(2)}) async-start(), calls=%async_computation.5 | async-start | bytes 3244032 | tf_op jit(solution)/shard_map/all_gather | solution.py:99
  496.2 4.1 copy-start.12
  497.7 2.6 copy-start.6
  601.4 5.1 copy-start.3
  619.3 5.1 copy-start.3
  626.1 1.8 copy-start.1
  (3 other events, 3.5 us)
Sparse Core Ops, SparseCore 0:
  30.3 130.1 all-gather.3
  163.0 124.2 all-gather.5
  484.5 11.6 reduce-scatter.1
  499.0 91.1 all-gather.7
